TPU v7x, 32 devices: a whole 2x2x4 slice. The times are simulated.
32 devices in a mesh: grp: 4 (over z), elem: 8 (over y, x, core).
Axes of the slice: x: 2, y: 2, z: 4, core: 2. Of those that a mesh axis runs over, the one named last changes fastest.
Arguments:
- state: float32 [8, 72, 8192], P(None, None, ('grp', 'elem')), may hold values from -6 to 6
- kappa: float32 [8192], P(('grp', 'elem')), may hold values from 0.08 to 0.8
- edge_nbrs: int32 [512, 4], P(('grp', 'elem')), may hold values from 0 to 511, as said below
- stencil: int32 [8192, 9], P(('grp', 'elem')), may hold values from 0 to 8191, as said below
- owner: int32 [8192], P(('grp', 'elem')), may hold values from -1 to 31, as said below
- w_first: bfloat16 [216, 256], replicated, may hold values from -0.75 to 0.75
- w_inner: bfloat16 [5, 768, 256], replicated, may hold values from -0.375 to 0.375
- w_last: bfloat16 [768, 8], replicated, may hold values from -0.375 to 0.375
Outputs:
- new_state: float32 [8, 72, 8192], P(None, None, ('grp', 'elem'))
Inputs may be any that keep to these rules, and one draw needn't show every extreme that they name: `edge_nbrs`: the neighbour across edge k of an element is held by the same device or by the device just before or after it along grp+elem, the last and the first device counting as adjacent; if e' is across edge k of e, then e is across edge (k + 2) mod 4 of e'. `stencil`: entry 4 of a column's block is the column itself; all nine entries name columns held by the same device. Every owner 0 to 31 is named by exactly 64 columns; the columns of one device name one owner at most 8 times, and in every draw some device names every owner exactly 8 times.
All inputs are finite; a program needn't handle non-finite values.
Results may differ from a plain program's by a relative error of at most 0.012.
Values may be sent and summed in bfloat16 or wider, within the bound.
No kernel may reach another device: no remote copies, remote signals or barrier semaphores. Data moves between devices by JAX's collectives and lax.ppermute only.
A program may use at most 64 MiB of HBM per device.

v0:
```python
import functools
import math

import jax
import jax.numpy as jnp
import numpy as np
from jax import lax
from jax.experimental import pallas as pl
from jax.experimental.pallas import tpu as pltpu
from jax.sharding import PartitionSpec as P

AXES = ("grp", "elem")
EDGE_NODES = ((1, 2), (7, 11), (14, 13), (8, 4))
VMEM = pl.BlockSpec(memory_space=pltpu.VMEM)
SMALL = pltpu.CompilerParams(vmem_limit_bytes=12 * 1024 * 1024)
SMEM = pl.BlockSpec(memory_space=pltpu.SMEM)
HIGHEST = lax.Precision.HIGHEST
BF16 = jnp.bfloat16
F32 = jnp.float32
NB = 32
STEP = 6
GROUP = 4


def second_derivative():
    points = np.array([-1.0, -math.sqrt(0.2), math.sqrt(0.2), 1.0])
    factors = np.array(
        [1.0 / np.prod([points[j] - points[m] for m in range(4) if m != j]) for j in range(4)]
    )
    deriv = np.zeros((4, 4))
    for i in range(4):
        for j in range(4):
            if i != j:
                deriv[i, j] = factors[j] / factors[i] / (points[i] - points[j])
        deriv[i, i] = -np.sum(deriv[i])
    return deriv @ deriv


def diffusion_matrix(columns):
    lap = second_derivative()
    eye = np.eye(4)
    node = np.einsum("ia,jb->abij", lap, eye) + np.einsum("ia,jb->abij", eye, lap)
    return np.kron(np.eye(columns // 16), node.reshape(16, 16)).astype(np.float32)


def edge_matrix(columns):
    sel = np.zeros((columns, columns // 2), np.float32)
    for e in range(columns // 16):
        for k in range(4):
            for m in range(2):
                sel[16 * e + EDGE_NODES[k][m], 8 * e + 2 * k + m] = 1
    return sel


def node_tables(columns):
    on_edge = np.zeros((4, columns), np.float32)
    offset = np.zeros((1, columns), np.float32)
    for k in range(4):
        for m in range(2):
            on_edge[k, EDGE_NODES[k][m] :: 16] = 1
            offset[0, EDGE_NODES[k][m] :: 16] = (k + 2) % 4 * 2 + 1 - m
    holder = np.kron(np.eye(columns // 16), np.ones((1, 16))).astype(np.float32)
    table = np.concatenate([on_edge, offset, np.zeros((3, columns), np.float32)], axis=0)
    return table, holder


def iota(shape, dim):
    return lax.broadcasted_iota(jnp.int32, shape, dim)


def silu(half):
    half = half.astype(BF16)
    return half + half * jnp.tanh(half)


def pack_kernel(dev_ref, state_ref, sten_ref, owner_ref, pay_ref):
    fields, levels, columns = state_ref.shape
    rows = fields * levels
    for l in range(0, levels, 2):
        pair = jnp.concatenate([state_ref[:, l, :], state_ref[:, l + 1, :]], axis=0)
        pay_ref[l * fields : (l + 2) * fields, :] = pair.astype(BF16)
    local = (sten_ref[...] - dev_ref[0] * columns).astype(F32)
    flag = jnp.where(owner_ref[...] >= 0, 1.0, 0.0)
    tail = jnp.concatenate([local, flag, jnp.zeros((6, columns), F32)], axis=0)
    pay_ref[rows : rows + 16, :] = tail.astype(BF16)


def edges_kernel(total, dev_ref, state_ref, kappa_ref, op_ref, sel_ref, nbr_ref, table_ref, holder_ref,
                 base_ref, edge_ref, facing_ref):
    fields, levels, columns = state_ref.shape
    elements = columns // 16
    flat = state_ref[...].reshape(fields * levels, columns)
    dyn = kappa_ref[...] * jnp.dot(flat, op_ref[...], precision=HIGHEST)
    edge = jnp.dot(dyn, sel_ref[...], precision=HIGHEST)
    edge_ref[...] = edge.astype(BF16)
    rel = lax.rem(nbr_ref[...] - (dev_ref[0] - 1) * elements + total, total).astype(F32)
    spread = jnp.dot(rel, holder_ref[...], precision=HIGHEST)
    on_edge = table_ref[0:4, :]
    is_edge = jnp.sum(on_edge, axis=0, keepdims=True)
    facing = 8.0 * jnp.sum(spread * on_edge, axis=0, keepdims=True) + table_ref[4:5, :]
    facing = jnp.where(is_edge > 0, facing, -1.0).astype(jnp.int32)
    facing_ref[...] = facing
    half = columns // 2
    pick = jnp.where(iota((half, columns), 0) + half == facing, 0.5, 0.0)
    own = jnp.dot(edge, pick, precision=HIGHEST)
    base_ref[...] = flat + (1.0 - 0.5 * is_edge) * dyn + own


def land(code, d, quota, columns):
    slot = jnp.where((code >= d * quota) & (code < (d + 1) * quota), code - d * quota, -2 * quota)
    spot = iota((2 * quota, columns), 0)
    return [jnp.where(spot == slot + h * quota, 1.0, 0.0).astype(BF16) for h in range(2)]


def middle_kernel(base_ref, low_ref, high_ref, facing_ref, out_ref):
    rows, columns = base_ref.shape
    half = columns // 2
    facing = facing_ref[...]
    acc = base_ref[...]
    for part, ref in ((0, low_ref), (2, high_ref)):
        pick = jnp.where(iota((half, columns), 0) + part * half == facing, 0.5, 0.0).astype(BF16)
        acc = acc + jnp.dot(ref[...], pick, preferred_element_type=F32)
    out_ref[...] = acc


def final_kernel(base_ref, code_ref, r0_ref, r1_ref, r2_ref, r3_ref, out_ref):
    fields, levels, columns = out_ref.shape
    quota = columns // GROUP
    code = code_ref[...]
    got = jnp.concatenate([r0_ref[...], r1_ref[...], r2_ref[...], r3_ref[...]], axis=1)
    puts = [land(code, d, quota, columns) for d in range(GROUP)]
    for h in range(2):
        put = jnp.concatenate([p[h] for p in puts], axis=0)
        physics = jnp.dot(got, put, preferred_element_type=F32)
        for i in range(levels // 2):
            l = h * (levels // 2) + i
            out_ref[:, l, :] = base_ref[:, l, :] + physics[i * fields : (i + 1) * fields, :]


def halve(y):
    y = y.reshape(y.shape[0] // 2, 2, *y.shape[1:])
    return (y[:, 0] + y[:, 1]) * BF16(0.5)


def widen(coarse, fine):
    step, cols, ch = coarse.shape
    return jnp.broadcast_to(coarse[:, None], (step, 2, cols, ch)).reshape(2 * step, cols, ch) + fine


def net_kernel(levels, fields, dev_ref, m0_ref, m1_ref, m2_ref, m3_ref, w1_ref, wi_ref, wl_ref,
               r0_ref, r1_ref, r2_ref, r3_ref, code_ref,
               oh_ref, g_ref, net_ref, w1s_ref, w_ref, first_ref, second_ref, pool2_ref, third_ref,
               pool3_ref, join3_ref, join2_ref, top_ref, p_ref, acc_ref, to_ref):
    rows = fields * levels
    columns = m0_ref.shape[1]
    quota = columns // GROUP
    wide = GROUP * columns
    ch = wi_ref.shape[2]
    taps = 9 * fields
    half2, half3 = levels // 2, levels // 4

    for ref, n in ((first_ref, levels), (pool2_ref, half2), (pool3_ref, half3), (join3_ref, half2),
                   (join2_ref, levels)):
        zero = jnp.zeros(ref.shape[1:], BF16)
        ref[0] = zero
        ref[n + 1] = zero
    net_ref[0] = jnp.zeros(net_ref.shape[1:], BF16)
    net_ref[levels + 1] = jnp.zeros(net_ref.shape[1:], BF16)
    net_ref[:, :, 80:128] = jnp.zeros((levels + 2, columns, 48), BF16)
    p_ref[:, 0:128] = jnp.zeros((24, 128), F32)
    p_ref[:, levels * NB + 128 :] = jnp.zeros((24, 128), F32)
    acc_ref[...] = jnp.zeros(acc_ref.shape, BF16)
    w1s_ref[...] = jnp.zeros(w1s_ref.shape, BF16)
    for t in range(3):
        w1s_ref[128 * t : 128 * t + taps, :] = w1_ref[taps * t : taps * (t + 1), :] * BF16(0.5)
    w_ref[...] = wi_ref[...] * BF16(0.5)
    w24 = jnp.concatenate([wl_ref[:, ch * t : ch * (t + 1)].astype(F32) for t in range(3)], axis=0).astype(BF16)

    me = lax.rem(dev_ref[0], GROUP)
    members = (m0_ref, m1_ref, m2_ref, m3_ref)
    upto = jnp.where(iota((columns, columns), 0) < iota((columns, columns), 1), 1.0, 0.0).astype(BF16)
    metas = [ref[rows : rows + 16, :] for ref in members]
    flags = [meta.astype(F32)[9:10, :] for meta in metas]
    counts = [jnp.sum(flag, axis=1, keepdims=True) for flag in flags]
    ranks, targets, active = [], [], jnp.zeros((1, 1), F32)
    for d in range(GROUP):
        start = jnp.zeros((1, 1), F32)
        for other in range(GROUP):
            start = start + jnp.where((me ^ other) < (me ^ d), counts[other], 0.0)
        local = jnp.dot(metas[d], upto, preferred_element_type=F32)[9:10, :].astype(jnp.int32)
        rank = local + start.astype(jnp.int32)
        ranks.append(jnp.where(flags[d] > 0, rank, -1))
        targets.append(jnp.where(flags[d] > 0, d * quota + local // GROUP + 1, 0).astype(F32))
        if d == 0:
            code_ref[...] = jnp.where(flags[d] > 0, (lax.rem(rank, GROUP) ^ me) * quota + local // GROUP, -1)
        active = active + counts[d]
    meta = jnp.concatenate(metas, axis=1)
    rank = jnp.concatenate(ranks, axis=1)
    share = (jnp.sum(active).astype(jnp.int32) - me + GROUP - 1) // GROUP
    slot = GROUP * iota((columns, wide), 0) + me
    choose = jnp.where(slot == rank, 1.0, 0.0).astype(BF16)
    flip = (((1,), (1,)), ((), ()))
    sten = lax.dot_general(meta, choose, flip, preferred_element_type=F32)
    part = (iota((16, wide), 1) // columns).astype(F32).astype(BF16)
    part = lax.dot_general(part, choose, flip, preferred_element_type=F32)
    sten = (sten + columns * part).astype(jnp.int32)
    target = jnp.broadcast_to(jnp.concatenate(targets, axis=1), (128, wide)).astype(BF16)
    to = lax.dot_general(choose, target, flip, preferred_element_type=F32).astype(jnp.int32) - 1
    to_ref[...] = jnp.where(to >= 0, to // quota * (2 * quota) + lax.rem(to, quota), -1)

    @pl.loop(0, (share + 127) // 128)
    def _(q):
        lanes = pl.ds(pl.multiple_of(q * 128, 128), 128)
        for k in range(9):
            for half in range(columns // 128):
                here = sten[k : k + 1, half * 128 : (half + 1) * 128]
                picked = here if half == 0 else jnp.where(q == half, here, picked)
            oh_ref[:, k * 128 : (k + 1) * 128] = jnp.where(iota((wide, 128), 0) == picked, 1.0, 0.0).astype(BF16)
        for k in range(0, 9, 2):
            n = 2 if k < 8 else 1
            got = jnp.dot(jnp.concatenate([ref[0:rows, :] for ref in members], axis=1), oh_ref[:, k * 128 : (k + n) * 128], preferred_element_type=F32)
            parts = [got[:, u * 128 : (u + 1) * 128].reshape(levels, fields, 128) for u in range(n)]
            if n == 1:
                parts.append(jnp.zeros_like(parts[0]))
            g_ref[0:levels, k * 8 : k * 8 + 16, :] = jnp.concatenate(parts, axis=1).astype(BF16)

        for l in range(levels):
            net_ref[l + 1, lanes, 0:80] = g_ref[l].T

    mask = jnp.where(iota((128 // NB * 8, 128), 0) // 8 == iota((128 // NB * 8, 128), 1) // NB, 1.0, 0.0)

    @pl.loop(0, (share + NB - 1) // NB)
    def _(b):
        c0 = pl.multiple_of(b * NB, NB)

        def conv(load, weight, n, emit):
            step = max(s for s in range(1, STEP + 1) if n % s == 0)
            for l0 in range(0, n, step):
                x = [load(l0 + t, step).reshape(step * NB, -1) for t in range(3)]
                acc = jnp.dot(jnp.concatenate(x, axis=1), weight, preferred_element_type=F32)
                emit(l0, step, silu(acc).reshape(step, NB, ch))

        def emit_first(l0, step, y):
            first_ref[l0 + 1 : l0 + 1 + step] = y

        def emit_second(l0, step, y):
            second_ref[l0 : l0 + step] = y
            pool2_ref[l0 // 2 + 1 : l0 // 2 + 1 + step // 2] = halve(y)

        def emit_third(l0, step, y):
            third_ref[l0 : l0 + step] = y
            pool3_ref[l0 // 2 + 1 : l0 // 2 + 1 + step // 2] = halve(y)

        def emit_deepest(l0, step, y):
            fine = third_ref[2 * l0 : 2 * (l0 + step)]
            join3_ref[2 * l0 + 1 : 2 * (l0 + step) + 1] = widen(y, fine)

        def emit_upper(l0, step, y):
            fine = second_ref[2 * l0 : 2 * (l0 + step)]
            join2_ref[2 * l0 + 1 : 2 * (l0 + step) + 1] = widen(y, fine)

        def emit_top(l0, step, y):
            top_ref[l0 : l0 + step] = y

        conv(lambda l, n: net_ref[l : l + n, pl.ds(c0, NB), :], w1s_ref[...], levels, emit_first)
        conv(lambda l, n: first_ref[l : l + n], w_ref[0], levels, emit_second)
        conv(lambda l, n: pool2_ref[l : l + n], w_ref[1], half2, emit_third)
        conv(lambda l, n: pool3_ref[l : l + n], w_ref[2], half3, emit_deepest)
        conv(lambda l, n: join3_ref[l : l + n], w_ref[3], half2, emit_upper)
        conv(lambda l, n: join2_ref[l : l + n], w_ref[4], levels, emit_top)

        group = 384
        for i in range(0, levels * NB, group):
            x = top_ref[i // NB : (i + group) // NB].reshape(group, ch)
            p_ref[:, i + 128 : i + group + 128] = lax.dot_general(w24, x, flip, preferred_element_type=F32)
        n = levels * NB
        out = p_ref[0:8, 128 - NB : n + 128 - NB] + p_ref[8:16, 128 : n + 128] + p_ref[16:24, 128 + NB : n + 128 + NB]
        tiles = []
        for i in range(n // 128):
            tile = out[:, i * 128 : (i + 1) * 128]
            tiles.append(jnp.concatenate([tile] * (128 // NB), axis=0) * mask)
        flat = jnp.concatenate(tiles, axis=0).astype(BF16)
        to = to_ref[pl.ds(c0, NB), :]
        place = []
        for h in range(2):
            lane = jnp.concatenate([to + jnp.where(to >= 0, h * quota, 0)] * (128 // NB), axis=0)
            hits = [jnp.where(lane == iota((128, 128), 1) + i * 128, 1.0, 0.0) for i in range(2 * columns // 128)]
            place.append(jnp.concatenate(hits, axis=1).astype(BF16))
        both = jnp.concatenate([flat[: rows // 2], flat[rows // 2 :]], axis=1)
        acc_ref[...] += jnp.dot(both, jnp.concatenate(place, axis=0), preferred_element_type=F32).astype(BF16)

    for d, ref in enumerate((r0_ref, r1_ref, r2_ref, r3_ref)):
        ref[...] = acc_ref[:, d * 2 * quota : (d + 1) * 2 * quota]


def per_device(state, kappa, edge_nbrs, stencil, owner, w_first, w_inner, w_last):
    fields, levels, columns = state.shape
    rows = fields * levels
    ch = w_inner.shape[2]
    devices = lax.axis_size(AXES)
    device = lax.axis_index(AXES)
    total = columns // 16 * devices
    dev = device.astype(jnp.int32).reshape(1)
    table, holder = node_tables(columns)
    f32 = functools.partial(jax.ShapeDtypeStruct, dtype=F32)
    bf16 = functools.partial(jax.ShapeDtypeStruct, dtype=BF16)
    i32 = functools.partial(jax.ShapeDtypeStruct, dtype=jnp.int32)

    payload = pl.pallas_call(
        pack_kernel,
        out_shape=bf16((rows + 16, columns)),
        in_specs=[SMEM] + [VMEM] * 3,
        out_specs=VMEM,
        name="pack",
    )(dev, state, stencil.T, owner.reshape(1, columns))
    def trade(x, d):
        return lax.ppermute(x, AXES, [(i, i ^ d) for i in range(devices)])

    member1 = trade(payload, 1)
    member2 = trade(payload, 2)

    base, edges, facing = pl.pallas_call(
        functools.partial(edges_kernel, total),
        out_shape=(f32((rows, columns)), bf16((rows, columns // 2)), i32((1, columns))),
        in_specs=[SMEM] + [VMEM] * 7,
        out_specs=(VMEM, VMEM, VMEM),
        cost_estimate=pl.CostEstimate(flops=3 * 10**9, bytes_accessed=2**21, transcendentals=0),
        name="edges",
    )(dev, state, kappa.reshape(1, columns), jnp.asarray(diffusion_matrix(columns)),
      jnp.asarray(edge_matrix(columns)), edge_nbrs.T, jnp.asarray(table), jnp.asarray(holder))

    member2, base = lax.optimization_barrier((member2, base))
    member3 = trade(member2, 1)
    low = lax.ppermute(edges, AXES, [(i, (i + 1) % devices) for i in range(devices)])
    high = lax.ppermute(edges, AXES, [(i, (i - 1) % devices) for i in range(devices)])

    bf = lambda *shape: pltpu.VMEM(shape, BF16)
    lanes = 2 * columns // GROUP
    *results, code = pl.pallas_call(
        functools.partial(net_kernel, levels, fields),
        out_shape=[bf16((rows // 2, lanes))] * GROUP + [i32((1, columns))],
        in_specs=[SMEM] + [VMEM] * (GROUP + 1) + [VMEM] * 2,
        out_specs=[VMEM] * (GROUP + 1),
        scratch_shapes=[
            bf(GROUP * columns, 9 * 128),
            bf(levels, 80, 128),
            bf(levels + 2, columns, 128),
            bf(3 * 128, ch),
            bf(*w_inner.shape),
            bf(levels + 2, NB, ch),
            bf(levels, NB, ch),
            bf(levels // 2 + 2, NB, ch),
            bf(levels // 2, NB, ch),
            bf(levels // 4 + 2, NB, ch),
            bf(levels // 2 + 2, NB, ch),
            bf(levels + 2, NB, ch),
            bf(levels, NB, ch),
            pltpu.VMEM((24, levels * NB + 256), F32),
            bf(rows // 2, GROUP * lanes),
            pltpu.VMEM((columns, 128), jnp.int32),
        ],
        compiler_params=pltpu.CompilerParams(vmem_limit_bytes=30 * 1024 * 1024),
        cost_estimate=pl.CostEstimate(flops=10**10, bytes_accessed=2**22, transcendentals=10**7),
        name="network",
    )(dev, payload, member1, member2, member3, w_first, w_inner, w_last.T)
    back = [trade(results[d], d) for d in (3, 2, 1)][::-1]

    middle = pl.pallas_call(
        middle_kernel,
        out_shape=f32((rows, columns)),
        in_specs=[VMEM] * 4,
        out_specs=VMEM,
        cost_estimate=pl.CostEstimate(flops=10**9, bytes_accessed=2**22, transcendentals=0),
        compiler_params=SMALL,
        name="middle",
    )(*lax.optimization_barrier((base, low, high, facing, results[0]))[:4])

    return pl.pallas_call(
        final_kernel,
        out_shape=f32((fields, levels, columns)),
        in_specs=[VMEM] * 6,
        out_specs=VMEM,
        compiler_params=SMALL,
        name="combine",
    )(middle.reshape(fields, levels, columns), code, results[0], *back)


def solution(mesh):
    in_specs = (
        P(None, None, AXES),
        P(AXES),
        P(AXES, None),
        P(AXES, None),
        P(AXES),
        P(),
        P(),
        P(),
    )
    return jax.shard_map(
        per_device, mesh=mesh, in_specs=in_specs, out_specs=P(None, None, AXES), check_vma=False
    )
```

profile of v0, /device:TPU:9, one launch (start us, length us, event | category | flops | bytes accessed | tf_op | source)
XLA Modules:
  0.0 51.4 jit_solution(10129930516370202186)
XLA Ops:
  0.0 2.0 %pack.1.m0_ref = bf16[592,256]{1,0:T(8,128)(2,1)} custom-call(s32[1]{0:T(128)} %bitcast.dev_ref, f32[8,72,256]{2,1,0:T(8,128)} %state_ref.3, s32[9,256]{1,0:T(8,128)} %bitcast.9, s32[1,256]{1,0:T(1,128)} %bitcast.10), custom_call_target="tpu_custom_call" | custom-call | tf_op jit(solution)/shard_map/pack/pallas_call | solution.py:309
  2.0 1.2 %collective-permute-start = (bf16[592,256]{1,0:T(8,128)(2,1)}, bf16[592,256]{1,0:T(8,128)(2,1)S(1)}, u32[]{:S(2)}, u32[]{:S(2)}) collective-permute-start(bf16[592,256]{1,0:T(8,128)(2,1)} %pack.1.m0_ref), channel_id=1, source_target_pairs={{0,2},{1,3},{2,0},{3,1},{4,6},{5,7},{6,4},{7,5},{8,10},{9,11},{10,... | collective-permute-start | bytes 909320 | tf_op jit(solution)/shard_map/ppermute | solution.py:317
  3.2 1.0 %collective-permute-start.3 = (bf16[592,256]{1,0:T(8,128)(2,1)}, bf16[592,256]{1,0:T(8,128)(2,1)S(1)}, u32[]{:S(2)}, u32[]{:S(2)}) collective-permute-start(bf16[592,256]{1,0:T(8,128)(2,1)} %pack.1.m0_ref), channel_id=1, source_target_pairs={{0,1},{1,0},{2,3},{3,2},{4,5},{5,4},{6,7},{7,6},{8,9},{9,8},{10,11... | collective-permute-start | bytes 909320 | tf_op jit(solution)/shard_map/ppermute | solution.py:317
  4.1 0.0 copy-start
  4.1 0.0 copy-start.1
  4.2 0.0 copy-start.2
  4.2 0.0 copy-start.3
  4.2 4.8 %edges.1 = (f32[576,256]{1,0:T(8,128)}, bf16[576,128]{1,0:T(8,128)(2,1)}, s32[1,256]{1,0:T(1,128)}) custom-call(s32[1]{0:T(128)} %bitcast.dev_ref, f32[8,72,256]{2,1,0:T(8,128)} %state_ref.3, f32[1,256]{1,0:T(1,128)} %bitcast.12, f32[256,256]{1,0:T(8,128)} %constant.18.clone.op_ref, f32[256,128]{1,0:T(8,128)} %constant.19.clone.sel_ref, s32[4,16]{1,0:T(4,128)} %bitcast.11, ...), custom_call_target="tpu_custom_call" | custom-call | flops 3000000000 | bytes 2097152 | tf_op jit(solution)/shard_map/edges/pallas_call | solution.py:322
  9.0 1.3 %collective-permute-done.m2_ref = bf16[592,256]{1,0:T(8,128)(2,1)S(1)} collective-permute-done((bf16[592,256]{1,0:T(8,128)(2,1)}, bf16[592,256]{1,0:T(8,128)(2,1)S(1)}, u32[]{:S(2)}, u32[]{:S(2)}) %collective-permute-start) | collective-permute-done | bytes 303136 | tf_op jit(solution)/shard_map/ppermute | solution.py:317
  10.2 1.5 %collective-permute-start.4 = (bf16[592,256]{1,0:T(8,128)(2,1)S(1)}, bf16[592,256]{1,0:T(8,128)(2,1)S(1)}, u32[]{:S(2)}, u32[]{:S(2)}) collective-permute-start(bf16[592,256]{1,0:T(8,128)(2,1)S(1)} %collective-permute-done.m2_ref), channel_id=1, source_target_pairs={{0,1},{1,0},{2,3},{3,2},{4,5},{5,4},{6,7},{7,6},{8,9},{9,8},{10,11... | collective-permute-start | bytes 909320 | tf_op jit(solution)/shard_map/ppermute | solution.py:317
  11.8 1.1 %collective-permute-start.1 = (bf16[576,128]{1,0:T(8,128)(2,1)}, bf16[576,128]{1,0:T(8,128)(2,1)S(1)}, u32[]{:S(2)}, u32[]{:S(2)}) collective-permute-start(bf16[576,128]{1,0:T(8,128)(2,1)} %get-tuple-element.21), channel_id=1, source_target_pairs={{0,1},{1,2},{2,3},{3,4},{4,5},{5,6},{6,7},{7,8},{8,9},{9,10},{10,1... | collective-permute-start | bytes 442376 | tf_op jit(solution)/shard_map/ppermute | solution.py:334
  12.9 0.0 collective-permute-start.2
  12.9 0.0 collective-permute-done.3.m1_ref
  12.9 0.1 collective-permute-done.4.m3_ref
  13.0 0.0 copy-done
  13.0 0.0 copy-done.1
  13.0 0.0 copy-done.2
  13.0 0.0 copy-done.3
  13.0 0.0 copy-start.4
  13.0 0.0 copy-start.5
  13.0 28.9 %network.1 = (bf16[288,128]{1,0:T(8,128)(2,1)S(1)}, bf16[288,128]{1,0:T(8,128)(2,1)S(1)}, bf16[288,128]{1,0:T(8,128)(2,1)S(1)}, bf16[288,128]{1,0:T(8,128)(2,1)S(1)}, s32[1,256]{1,0:T(1,128)S(1)}) custom-call(s32[1]{0:T(128)} %bitcast.dev_ref, bf16[592,256]{1,0:T(8,128)(2,1)S(1)} %copy-done, bf16[592,256]{1,0:T(8,128)(2,1)S(1)} %collective-permute-done.3.m1_ref, ...), custom_call_target="tpu_custom_call" | custom-call | flops 10000000000 | bytes 4194304 | tf_op jit(solution)/shard_map/network/pallas_call | solution.py:339
  42.0 0.0 collective-permute-done.1.low_ref
  42.0 0.0 collective-permute-done.2.high_ref
  42.0 2.4 %collective-permute-start.5 = (bf16[288,128]{1,0:T(8,128)(2,1)S(1)}, bf16[288,128]{1,0:T(8,128)(2,1)S(1)}, u32[]{:S(2)}, u32[]{:S(2)}) collective-permute-start(bf16[288,128]{1,0:T(8,128)(2,1)S(1)} %get-tuple-element.30), channel_id=1, source_target_pairs={{0,1},{1,0},{2,3},{3,2},{4,5},{5,4},{6,7},{7,6},{8,9},{9,8},{10,11... | collective-permute-start | bytes 221192 | tf_op jit(solution)/shard_map/ppermute | solution.py:317
  44.4 0.0 collective-permute-start.6
  44.4 1.7 %collective-permute-start.7 = (bf16[288,128]{1,0:T(8,128)(2,1)S(1)}, bf16[288,128]{1,0:T(8,128)(2,1)S(1)}, u32[]{:S(2)}, u32[]{:S(2)}) collective-permute-start(bf16[288,128]{1,0:T(8,128)(2,1)S(1)} %get-tuple-element.32), channel_id=1, source_target_pairs={{0,3},{1,2},{2,1},{3,0},{4,7},{5,6},{6,5},{7,4},{8,11},{9,10},{10,... | collective-permute-start | bytes 221192 | tf_op jit(solution)/shard_map/ppermute | solution.py:317
  46.1 0.0 copy-done.4
  46.1 0.0 copy-done.5
  46.1 0.3 middle.1
  46.4 0.0 collective-permute-done.5.r1_ref
  46.4 1.8 %collective-permute-done.6.r2_ref = bf16[288,128]{1,0:T(8,128)(2,1)S(1)} collective-permute-done((bf16[288,128]{1,0:T(8,128)(2,1)S(1)}, bf16[288,128]{1,0:T(8,128)(2,1)S(1)}, u32[]{:S(2)}, u32[]{:S(2)}) %collective-permute-start.6) | collective-permute-done | bytes 73760 | tf_op jit(solution)/shard_map/ppermute | solution.py:317
  48.2 1.7 %collective-permute-done.7.r3_ref = bf16[288,128]{1,0:T(8,128)(2,1)S(1)} collective-permute-done((bf16[288,128]{1,0:T(8,128)(2,1)S(1)}, bf16[288,128]{1,0:T(8,128)(2,1)S(1)}, u32[]{:S(2)}, u32[]{:S(2)}) %collective-permute-start.7) | collective-permute-done | bytes 73760 | tf_op jit(solution)/shard_map/ppermute | solution.py:317
  50.0 1.4 %combine.1 = f32[8,72,256]{2,1,0:T(8,128)} custom-call(f32[8,72,256]{2,1,0:T(8,128)S(1)} %bitcast.7, s32[1,256]{1,0:T(1,128)S(1)} %get-tuple-element.29.code_ref, bf16[288,128]{1,0:T(8,128)(2,1)S(1)} %get-tuple-element.24.r0_ref, bf16[288,128]{1,0:T(8,128)(2,1)S(1)} %collective-permute-done.5.r1_ref, bf16[288,128]{1,0:T(8,128)(2,1)S(1)} %collective-permute-done.6.r2_ref, ...), custom_call_target="tpu_custom_call" | custom-call | tf_op jit(solution)/shard_map/combine/pallas_call | solution.py:378
Async XLA Ops:
  2.0 8.3 %collective-permute-start = (bf16[592,256]{1,0:T(8,128)(2,1)}, bf16[592,256]{1,0:T(8,128)(2,1)S(1)}, u32[]{:S(2)}, u32[]{:S(2)}) collective-permute-start(bf16[592,256]{1,0:T(8,128)(2,1)} %pack.1.m0_ref), channel_id=1, source_target_pairs={{0,2},{1,3},{2,0},{3,1},{4,6},{5,7},{6,4},{7,5},{8,10},{9,11},{10,... | collective-permute-start | bytes 909320 | tf_op jit(solution)/shard_map/ppermute | solution.py:317
  3.2 9.7 %collective-permute-start.3 = (bf16[592,256]{1,0:T(8,128)(2,1)}, bf16[592,256]{1,0:T(8,128)(2,1)S(1)}, u32[]{:S(2)}, u32[]{:S(2)}) collective-permute-start(bf16[592,256]{1,0:T(8,128)(2,1)} %pack.1.m0_ref), channel_id=1, source_target_pairs={{0,1},{1,0},{2,3},{3,2},{4,5},{5,4},{6,7},{7,6},{8,9},{9,8},{10,11... | collective-permute-start | bytes 909320 | tf_op jit(solution)/shard_map/ppermute | solution.py:317
  4.1 8.9 %copy-start = (bf16[592,256]{1,0:T(8,128)(2,1)S(1)}, bf16[592,256]{1,0:T(8,128)(2,1)}, u32[]{:S(2)}) copy-start(bf16[592,256]{1,0:T(8,128)(2,1)} %pack.1.m0_ref) | copy-start | bytes 909316
  4.1 8.9 %copy-start.1 = (bf16[5,768,256]{2,1,0:T(8,128)(2,1)S(1)}, bf16[5,768,256]{2,1,0:T(8,128)(2,1)}, u32[]{:S(2)}) copy-start(bf16[5,768,256]{2,1,0:T(8,128)(2,1)} %wi_ref.1) | copy-start | bytes 5898244
  4.2 8.9 %copy-start.2 = (bf16[216,256]{1,0:T(8,128)(2,1)S(1)}, bf16[216,256]{1,0:T(8,128)(2,1)}, u32[]{:S(2)}) copy-start(bf16[216,256]{1,0:T(8,128)(2,1)} %w1_ref.1) | copy-start | bytes 331780
  4.2 8.9 %copy-start.3 = (bf16[768,8]{0,1:T(8,128)(2,1)S(1)}, bf16[768,8]{0,1:T(8,128)(2,1)}, u32[]{:S(2)}) copy-start(bf16[768,8]{0,1:T(8,128)(2,1)} %param.19) | copy-start | bytes 36868
  10.2 2.8 %collective-permute-start.4 = (bf16[592,256]{1,0:T(8,128)(2,1)S(1)}, bf16[592,256]{1,0:T(8,128)(2,1)S(1)}, u32[]{:S(2)}, u32[]{:S(2)}) collective-permute-start(bf16[592,256]{1,0:T(8,128)(2,1)S(1)} %collective-permute-done.m2_ref), channel_id=1, source_target_pairs={{0,1},{1,0},{2,3},{3,2},{4,5},{5,4},{6,7},{7,6},{8,9},{9,8},{10,11... | collective-permute-start | bytes 909320 | tf_op jit(solution)/shard_map/ppermute | solution.py:317
  11.8 30.2 %collective-permute-start.1 = (bf16[576,128]{1,0:T(8,128)(2,1)}, bf16[576,128]{1,0:T(8,128)(2,1)S(1)}, u32[]{:S(2)}, u32[]{:S(2)}) collective-permute-start(bf16[576,128]{1,0:T(8,128)(2,1)} %get-tuple-element.21), channel_id=1, source_target_pairs={{0,1},{1,2},{2,3},{3,4},{4,5},{5,6},{6,7},{7,8},{8,9},{9,10},{10,1... | collective-permute-start | bytes 442376 | tf_op jit(solution)/shard_map/ppermute | solution.py:334
  12.9 29.1 %collective-permute-start.2 = (bf16[576,128]{1,0:T(8,128)(2,1)}, bf16[576,128]{1,0:T(8,128)(2,1)S(1)}, u32[]{:S(2)}, u32[]{:S(2)}) collective-permute-start(bf16[576,128]{1,0:T(8,128)(2,1)} %get-tuple-element.21), channel_id=1, source_target_pairs={{0,31},{1,0},{2,1},{3,2},{4,3},{5,4},{6,5},{7,6},{8,7},{9,8},{10,9... | collective-permute-start | bytes 442376 | tf_op jit(solution)/shard_map/ppermute | solution.py:335
  13.0 33.1 %copy-start.4 = (f32[576,256]{1,0:T(8,128)S(1)}, f32[576,256]{1,0:T(8,128)}, u32[]{:S(2)}) copy-start(f32[576,256]{1,0:T(8,128)} %get-tuple-element.25.base_ref) | copy-start | bytes 1769476
  13.0 33.1 %copy-start.5 = (s32[1,256]{1,0:T(1,128)S(1)}, s32[1,256]{1,0:T(1,128)}, u32[]{:S(2)}) copy-start(s32[1,256]{1,0:T(1,128)} %get-tuple-element.28.facing_ref) | copy-start | bytes 3076
  42.0 4.4 %collective-permute-start.5 = (bf16[288,128]{1,0:T(8,128)(2,1)S(1)}, bf16[288,128]{1,0:T(8,128)(2,1)S(1)}, u32[]{:S(2)}, u32[]{:S(2)}) collective-permute-start(bf16[288,128]{1,0:T(8,128)(2,1)S(1)} %get-tuple-element.30), channel_id=1, source_target_pairs={{0,1},{1,0},{2,3},{3,2},{4,5},{5,4},{6,7},{7,6},{8,9},{9,8},{10,11... | collective-permute-start | bytes 221192 | tf_op jit(solution)/shard_map/ppermute | solution.py:317
  44.4 3.8 %collective-permute-start.6 = (bf16[288,128]{1,0:T(8,128)(2,1)S(1)}, bf16[288,128]{1,0:T(8,128)(2,1)S(1)}, u32[]{:S(2)}, u32[]{:S(2)}) collective-permute-start(bf16[288,128]{1,0:T(8,128)(2,1)S(1)} %get-tuple-element.31), channel_id=1, source_target_pairs={{0,2},{1,3},{2,0},{3,1},{4,6},{5,7},{6,4},{7,5},{8,10},{9,11},{10,... | collective-permute-start | bytes 221192 | tf_op jit(solution)/shard_map/ppermute | solution.py:317
  44.4 5.6 %collective-permute-start.7 = (bf16[288,128]{1,0:T(8,128)(2,1)S(1)}, bf16[288,128]{1,0:T(8,128)(2,1)S(1)}, u32[]{:S(2)}, u32[]{:S(2)}) collective-permute-start(bf16[288,128]{1,0:T(8,128)(2,1)S(1)} %get-tuple-element.32), channel_id=1, source_target_pairs={{0,3},{1,2},{2,1},{3,0},{4,7},{5,6},{6,5},{7,4},{8,11},{9,10},{10,... | collective-permute-start | bytes 221192 | tf_op jit(solution)/shard_map/ppermute | solution.py:317
where the time goes:
time: 51.1 us; the launch traced here: 51.4 us
  Pallas kernels  37.4 us (73%)
  starting transfers between devices  8.94 us (17%)
  waiting for transfers between devices  4.94 us (10%)
    pallas_call x1, Pallas kernels, per_device(): pl.pallas_call(functools.partial(net_kernel, levels, fields), out_shape=[...  28.9 us
    ppermute x6, starting transfers between devices, trade(): return lax.ppermute(x, AXES, [(i, i ^ d) for i in range(devices)])  7.84 us
    ppermute x6, waiting for transfers between devices, trade(): return lax.ppermute(x, AXES, [(i, i ^ d) for i in range(devices)])  4.93 us
    pallas_call x1, Pallas kernels, per_device(): pl.pallas_call(functools.partial(edges_kernel, total), out_shape=(f32((ro...  4.83 us
    pallas_call x1, Pallas kernels, per_device(): pl.pallas_call(pack_kernel, out_shape=bf16((rows + 16, columns)), in_spec...  1.98 us
    pallas_call x1, Pallas kernels, per_device(): pl.pallas_call(final_kernel, out_shape=f32((fields, levels, columns)), in...  1.43 us
    ppermute x1, starting transfers between devices, per_device(): lax.ppermute(edges, AXES, [(i, (i + 1) % devices) for i in range(devices)])  1.1 us
  transfers between devices with their start and end apart: 8, of which 4 were waited for; matrix products, arithmetic and copies ran while one was open for 0% of the time, Pallas kernels for 66%

commit v1 on v0

--- a/solution.py
+++ b/solution.py
@@ -18,7 +18,7 @@
 BF16 = jnp.bfloat16
 F32 = jnp.float32
 NB = 32
-STEP = 6
+STEP = 12
 GROUP = 4
 
 
@@ -69,8 +69,7 @@
 
 
 def silu(half):
-    half = half.astype(BF16)
-    return half + half * jnp.tanh(half)
+    return (half + half * jnp.tanh(half)).astype(BF16)
 
 
 def pack_kernel(dev_ref, state_ref, sten_ref, owner_ref, pay_ref):
@@ -173,7 +172,13 @@
     w1s_ref[...] = jnp.zeros(w1s_ref.shape, BF16)
     for t in range(3):
         w1s_ref[128 * t : 128 * t + taps, :] = w1_ref[taps * t : taps * (t + 1), :] * BF16(0.5)
-    w_ref[...] = wi_ref[...] * BF16(0.5)
+    for i in range(wi_ref.shape[0]):
+        g = [wi_ref[i, ch * t : ch * (t + 1), :].astype(F32) for t in range(3)]
+        sides, middle = 0.25 * (g[0] + g[2]), 0.25 * g[1]
+        w_ref[4 * i] = (0.5 * g[0]).astype(BF16)
+        w_ref[4 * i + 1] = (sides + middle).astype(BF16)
+        w_ref[4 * i + 2] = (sides - middle).astype(BF16)
+        w_ref[4 * i + 3] = (0.5 * g[2]).astype(BF16)
     w24 = jnp.concatenate([wl_ref[:, ch * t : ch * (t + 1)].astype(F32) for t in range(3)], axis=0).astype(BF16)
 
     me = lax.rem(dev_ref[0], GROUP)
@@ -233,12 +238,26 @@
     def _(b):
         c0 = pl.multiple_of(b * NB, NB)
 
-        def conv(load, weight, n, emit):
-            step = max(s for s in range(1, STEP + 1) if n % s == 0)
+        def conv_first(n, emit):
+            for l0 in range(0, n, STEP):
+                x = [net_ref[l0 + t : l0 + t + STEP, pl.ds(c0, NB), :].reshape(STEP * NB, 128) for t in range(3)]
+                acc = jnp.dot(jnp.concatenate(x, axis=1), w1s_ref[...], preferred_element_type=F32)
+                emit(l0, STEP, silu(acc).reshape(STEP, NB, ch))
+
+        def conv(src, layer, n, emit):
+            step = min(n, 2 * STEP)
+            while n % step or step % 2:
+                step -= 1
+            pairs = step // 2
             for l0 in range(0, n, step):
-                x = [load(l0 + t, step).reshape(step * NB, -1) for t in range(3)]
-                acc = jnp.dot(jnp.concatenate(x, axis=1), weight, preferred_element_type=F32)
-                emit(l0, step, silu(acc).reshape(step, NB, ch))
+                x = src[l0 : l0 + step + 2].reshape(pairs + 1, 2, NB, ch)
+                even, odd = x[:, 0], x[:, 1]
+                d0, d1, d2, d3 = even[:-1], odd[:-1], even[1:], odd[1:]
+                m = [jnp.dot(d.reshape(pairs * NB, ch), w_ref[4 * layer + i], preferred_element_type=F32)
+                     for i, d in enumerate((d0 - d2, d1 + d2, d2 - d1, d1 - d3))]
+                y = [silu(m[0] + (m[1] + m[2])), silu((m[1] - m[2]) - m[3])]
+                y = jnp.concatenate([v.reshape(pairs, 1, NB, ch) for v in y], axis=1)
+                emit(l0, step, y.reshape(step, NB, ch))
 
         def emit_first(l0, step, y):
             first_ref[l0 + 1 : l0 + 1 + step] = y
@@ -262,12 +281,12 @@
         def emit_top(l0, step, y):
             top_ref[l0 : l0 + step] = y
 
-        conv(lambda l, n: net_ref[l : l + n, pl.ds(c0, NB), :], w1s_ref[...], levels, emit_first)
-        conv(lambda l, n: first_ref[l : l + n], w_ref[0], levels, emit_second)
-        conv(lambda l, n: pool2_ref[l : l + n], w_ref[1], half2, emit_third)
-        conv(lambda l, n: pool3_ref[l : l + n], w_ref[2], half3, emit_deepest)
-        conv(lambda l, n: join3_ref[l : l + n], w_ref[3], half2, emit_upper)
-        conv(lambda l, n: join2_ref[l : l + n], w_ref[4], levels, emit_top)
+        conv_first(levels, emit_first)
+        conv(first_ref, 0, levels, emit_second)
+        conv(pool2_ref, 1, half2, emit_third)
+        conv(pool3_ref, 2, half3, emit_deepest)
+        conv(join3_ref, 3, half2, emit_upper)
+        conv(join2_ref, 4, levels, emit_top)
 
         group = 384
         for i in range(0, levels * NB, group):
@@ -346,7 +365,7 @@
             bf(levels, 80, 128),
             bf(levels + 2, columns, 128),
             bf(3 * 128, ch),
-            bf(*w_inner.shape),
+            bf(4 * w_inner.shape[0], ch, ch),
             bf(levels + 2, NB, ch),
             bf(levels, NB, ch),
             bf(levels // 2 + 2, NB, ch),

time: 51.1 us -> 47.7 us (0.933)
  the two profiles are of different devices: /device:TPU:9 before, /device:TPU:0 now
where the time goes in v1:
time: 47.7 us; the launch traced here: 47.6 us
  Pallas kernels  30.5 us (64%)
  starting transfers between devices  10.7 us (22%)
  waiting for transfers between devices  6.17 us (13%)
    pallas_call x1, Pallas kernels, per_device(): pl.pallas_call(functools.partial(net_kernel, levels, fields), out_shape=[...  22 us
    ppermute x6, waiting for transfers between devices, trade(): return lax.ppermute(x, AXES, [(i, i ^ d) for i in range(devices)])  6.17 us
    ppermute x1, starting transfers between devices, per_device(): lax.ppermute(edges, AXES, [(i, (i - 1) % devices) for i in range(devices)])  5.34 us
    ppermute x6, starting transfers between devices, trade(): return lax.ppermute(x, AXES, [(i, i ^ d) for i in range(devices)])  4.87 us
    pallas_call x1, Pallas kernels, per_device(): pl.pallas_call(functools.partial(edges_kernel, total), out_shape=(f32((ro...  4.83 us
    pallas_call x1, Pallas kernels, per_device(): pl.pallas_call(pack_kernel, out_shape=bf16((rows + 16, columns)), in_spec...  1.98 us
    pallas_call x1, Pallas kernels, per_device(): pl.pallas_call(final_kernel, out_shape=f32((fields, levels, columns)), in...  1.43 us
  transfers between devices with their start and end apart: 8, of which 3 were waited for; matrix products, arithmetic and copies ran while one was open for 0% of the time, Pallas kernels for 57%

profile of v1, /device:TPU:0, one launch (start us, length us, event | category | flops | bytes accessed | tf_op | source)
XLA Modules:
  0.0 47.6 jit_solution(13711359136118593162)
XLA Ops:
  0.0 2.0 %pack.1.m0_ref = bf16[592,256]{1,0:T(8,128)(2,1)} custom-call(s32[1]{0:T(128)} %bitcast.dev_ref, f32[8,72,256]{2,1,0:T(8,128)} %state_ref.3, s32[9,256]{1,0:T(8,128)} %bitcast.9, s32[1,256]{1,0:T(1,128)} %bitcast.10), custom_call_target="tpu_custom_call" | custom-call | tf_op jit(solution)/shard_map/pack/pallas_call | solution.py:328
  2.0 2.9 %collective-permute-start = (bf16[592,256]{1,0:T(8,128)(2,1)}, bf16[592,256]{1,0:T(8,128)(2,1)S(1)}, u32[]{:S(2)}, u32[]{:S(2)}) collective-permute-start(bf16[592,256]{1,0:T(8,128)(2,1)} %pack.1.m0_ref), channel_id=1, source_target_pairs={{0,2},{1,3},{2,0},{3,1},{4,6},{5,7},{6,4},{7,5},{8,10},{9,11},{10,... | collective-permute-start | bytes 909320 | tf_op jit(solution)/shard_map/ppermute | solution.py:336
  4.9 0.0 collective-permute-start.3
  4.9 0.0 copy-start
  4.9 0.0 copy-start.1
  4.9 0.0 copy-start.2
  4.9 0.0 copy-start.3
  4.9 4.8 %edges.1 = (f32[576,256]{1,0:T(8,128)}, bf16[576,128]{1,0:T(8,128)(2,1)}, s32[1,256]{1,0:T(1,128)}) custom-call(s32[1]{0:T(128)} %bitcast.dev_ref, f32[8,72,256]{2,1,0:T(8,128)} %state_ref.3, f32[1,256]{1,0:T(1,128)} %bitcast.12, f32[256,256]{1,0:T(8,128)} %constant.18.clone.op_ref, f32[256,128]{1,0:T(8,128)} %constant.19.clone.sel_ref, s32[4,16]{1,0:T(4,128)} %bitcast.11, ...), custom_call_target="tpu_custom_call" | custom-call | flops 3000000000 | bytes 2097152 | tf_op jit(solution)/shard_map/edges/pallas_call | solution.py:341
  9.8 2.5 %collective-permute-done.m2_ref = bf16[592,256]{1,0:T(8,128)(2,1)S(1)} collective-permute-done((bf16[592,256]{1,0:T(8,128)(2,1)}, bf16[592,256]{1,0:T(8,128)(2,1)S(1)}, u32[]{:S(2)}, u32[]{:S(2)}) %collective-permute-start) | collective-permute-done | bytes 303136 | tf_op jit(solution)/shard_map/ppermute | solution.py:336
  12.3 0.0 collective-permute-start.4
  12.3 0.5 %collective-permute-start.1 = (bf16[576,128]{1,0:T(8,128)(2,1)}, bf16[576,128]{1,0:T(8,128)(2,1)S(1)}, u32[]{:S(2)}, u32[]{:S(2)}) collective-permute-start(bf16[576,128]{1,0:T(8,128)(2,1)} %get-tuple-element.21), channel_id=1, source_target_pairs={{0,1},{1,2},{2,3},{3,4},{4,5},{5,6},{6,7},{7,8},{8,9},{9,10},{10,1... | collective-permute-start | bytes 442376 | tf_op jit(solution)/shard_map/ppermute | solution.py:353
  12.8 5.3 %collective-permute-start.2 = (bf16[576,128]{1,0:T(8,128)(2,1)}, bf16[576,128]{1,0:T(8,128)(2,1)S(1)}, u32[]{:S(2)}, u32[]{:S(2)}) collective-permute-start(bf16[576,128]{1,0:T(8,128)(2,1)} %get-tuple-element.21), channel_id=1, source_target_pairs={{0,31},{1,0},{2,1},{3,2},{4,3},{5,4},{6,5},{7,6},{8,7},{9,8},{10,9... | collective-permute-start | bytes 442376 | tf_op jit(solution)/shard_map/ppermute | solution.py:354
  18.2 0.0 collective-permute-done.3.m1_ref
  18.2 0.0 collective-permute-done.4.m3_ref
  18.2 0.0 copy-done
  18.2 0.0 copy-done.1
  18.2 0.0 copy-done.2
  18.2 0.0 copy-done.3
  18.2 0.0 copy-start.4
  18.2 0.0 copy-start.5
  18.2 22.0 %network.1 = (bf16[288,128]{1,0:T(8,128)(2,1)S(1)}, bf16[288,128]{1,0:T(8,128)(2,1)S(1)}, bf16[288,128]{1,0:T(8,128)(2,1)S(1)}, bf16[288,128]{1,0:T(8,128)(2,1)S(1)}, s32[1,256]{1,0:T(1,128)S(1)}) custom-call(s32[1]{0:T(128)} %bitcast.dev_ref, bf16[592,256]{1,0:T(8,128)(2,1)S(1)} %copy-done, bf16[592,256]{1,0:T(8,128)(2,1)S(1)} %collective-permute-done.3.m1_ref, ...), custom_call_target="tpu_custom_call" | custom-call | flops 10000000000 | bytes 4194304 | tf_op jit(solution)/shard_map/network/pallas_call | solution.py:358
  40.3 0.0 collective-permute-done.1.low_ref
  40.3 0.0 collective-permute-done.2.high_ref
  40.3 0.1 collective-permute-start.5
  40.4 0.1 collective-permute-start.6
  40.4 1.8 %collective-permute-start.7 = (bf16[288,128]{1,0:T(8,128)(2,1)S(1)}, bf16[288,128]{1,0:T(8,128)(2,1)S(1)}, u32[]{:S(2)}, u32[]{:S(2)}) collective-permute-start(bf16[288,128]{1,0:T(8,128)(2,1)S(1)} %get-tuple-element.32), channel_id=1, source_target_pairs={{0,3},{1,2},{2,1},{3,0},{4,7},{5,6},{6,5},{7,4},{8,11},{9,10},{10,... | collective-permute-start | bytes 221192 | tf_op jit(solution)/shard_map/ppermute | solution.py:336
  42.2 0.0 copy-done.4
  42.2 0.0 copy-done.5
  42.2 0.3 middle.1
  42.5 0.0 collective-permute-done.5.r1_ref
  42.5 2.9 %collective-permute-done.6.r2_ref = bf16[288,128]{1,0:T(8,128)(2,1)S(1)} collective-permute-done((bf16[288,128]{1,0:T(8,128)(2,1)S(1)}, bf16[288,128]{1,0:T(8,128)(2,1)S(1)}, u32[]{:S(2)}, u32[]{:S(2)}) %collective-permute-start.6) | collective-permute-done | bytes 73760 | tf_op jit(solution)/shard_map/ppermute | solution.py:336
  45.5 0.7 %collective-permute-done.7.r3_ref = bf16[288,128]{1,0:T(8,128)(2,1)S(1)} collective-permute-done((bf16[288,128]{1,0:T(8,128)(2,1)S(1)}, bf16[288,128]{1,0:T(8,128)(2,1)S(1)}, u32[]{:S(2)}, u32[]{:S(2)}) %collective-permute-start.7) | collective-permute-done | bytes 73760 | tf_op jit(solution)/shard_map/ppermute | solution.py:336
  46.2 1.4 %combine.1 = f32[8,72,256]{2,1,0:T(8,128)} custom-call(f32[8,72,256]{2,1,0:T(8,128)S(1)} %bitcast.7, s32[1,256]{1,0:T(1,128)S(1)} %get-tuple-element.29.code_ref, bf16[288,128]{1,0:T(8,128)(2,1)S(1)} %get-tuple-element.24.r0_ref, bf16[288,128]{1,0:T(8,128)(2,1)S(1)} %collective-permute-done.5.r1_ref, bf16[288,128]{1,0:T(8,128)(2,1)S(1)} %collective-permute-done.6.r2_ref, ...), custom_call_target="tpu_custom_call" | custom-call | tf_op jit(solution)/shard_map/combine/pallas_call | solution.py:397
Async XLA Ops:
  2.0 10.3 %collective-permute-start = (bf16[592,256]{1,0:T(8,128)(2,1)}, bf16[592,256]{1,0:T(8,128)(2,1)S(1)}, u32[]{:S(2)}, u32[]{:S(2)}) collective-permute-start(bf16[592,256]{1,0:T(8,128)(2,1)} %pack.1.m0_ref), channel_id=1, source_target_pairs={{0,2},{1,3},{2,0},{3,1},{4,6},{5,7},{6,4},{7,5},{8,10},{9,11},{10,... | collective-permute-start | bytes 909320 | tf_op jit(solution)/shard_map/ppermute | solution.py:336
  4.9 13.2 %collective-permute-start.3 = (bf16[592,256]{1,0:T(8,128)(2,1)}, bf16[592,256]{1,0:T(8,128)(2,1)S(1)}, u32[]{:S(2)}, u32[]{:S(2)}) collective-permute-start(bf16[592,256]{1,0:T(8,128)(2,1)} %pack.1.m0_ref), channel_id=1, source_target_pairs={{0,1},{1,0},{2,3},{3,2},{4,5},{5,4},{6,7},{7,6},{8,9},{9,8},{10,11... | collective-permute-start | bytes 909320 | tf_op jit(solution)/shard_map/ppermute | solution.py:336
  4.9 13.3 %copy-start = (bf16[592,256]{1,0:T(8,128)(2,1)S(1)}, bf16[592,256]{1,0:T(8,128)(2,1)}, u32[]{:S(2)}) copy-start(bf16[592,256]{1,0:T(8,128)(2,1)} %pack.1.m0_ref) | copy-start | bytes 909316
  4.9 13.3 %copy-start.1 = (bf16[5,768,256]{2,1,0:T(8,128)(2,1)S(1)}, bf16[5,768,256]{2,1,0:T(8,128)(2,1)}, u32[]{:S(2)}) copy-start(bf16[5,768,256]{2,1,0:T(8,128)(2,1)} %wi_ref.1) | copy-start | bytes 5898244
  4.9 13.3 %copy-start.2 = (bf16[216,256]{1,0:T(8,128)(2,1)S(1)}, bf16[216,256]{1,0:T(8,128)(2,1)}, u32[]{:S(2)}) copy-start(bf16[216,256]{1,0:T(8,128)(2,1)} %w1_ref.1) | copy-start | bytes 331780
  4.9 13.3 %copy-start.3 = (bf16[768,8]{0,1:T(8,128)(2,1)S(1)}, bf16[768,8]{0,1:T(8,128)(2,1)}, u32[]{:S(2)}) copy-start(bf16[768,8]{0,1:T(8,128)(2,1)} %param.19) | copy-start | bytes 36868
  12.3 5.9 %collective-permute-start.4 = (bf16[592,256]{1,0:T(8,128)(2,1)S(1)}, bf16[592,256]{1,0:T(8,128)(2,1)S(1)}, u32[]{:S(2)}, u32[]{:S(2)}) collective-permute-start(bf16[592,256]{1,0:T(8,128)(2,1)S(1)} %collective-permute-done.m2_ref), channel_id=1, source_target_pairs={{0,1},{1,0},{2,3},{3,2},{4,5},{5,4},{6,7},{7,6},{8,9},{9,8},{10,11... | collective-permute-start | bytes 909320 | tf_op jit(solution)/shard_map/ppermute | solution.py:336
  12.3 27.9 %collective-permute-start.1 = (bf16[576,128]{1,0:T(8,128)(2,1)}, bf16[576,128]{1,0:T(8,128)(2,1)S(1)}, u32[]{:S(2)}, u32[]{:S(2)}) collective-permute-start(bf16[576,128]{1,0:T(8,128)(2,1)} %get-tuple-element.21), channel_id=1, source_target_pairs={{0,1},{1,2},{2,3},{3,4},{4,5},{5,6},{6,7},{7,8},{8,9},{9,10},{10,1... | collective-permute-start | bytes 442376 | tf_op jit(solution)/shard_map/ppermute | solution.py:353
  12.8 27.4 %collective-permute-start.2 = (bf16[576,128]{1,0:T(8,128)(2,1)}, bf16[576,128]{1,0:T(8,128)(2,1)S(1)}, u32[]{:S(2)}, u32[]{:S(2)}) collective-permute-start(bf16[576,128]{1,0:T(8,128)(2,1)} %get-tuple-element.21), channel_id=1, source_target_pairs={{0,31},{1,0},{2,1},{3,2},{4,3},{5,4},{6,5},{7,6},{8,7},{9,8},{10,9... | collective-permute-start | bytes 442376 | tf_op jit(solution)/shard_map/ppermute | solution.py:354
  18.2 24.0 %copy-start.4 = (f32[576,256]{1,0:T(8,128)S(1)}, f32[576,256]{1,0:T(8,128)}, u32[]{:S(2)}) copy-start(f32[576,256]{1,0:T(8,128)} %get-tuple-element.25.base_ref) | copy-start | bytes 1769476
  18.2 24.0 %copy-start.5 = (s32[1,256]{1,0:T(1,128)S(1)}, s32[1,256]{1,0:T(1,128)}, u32[]{:S(2)}) copy-start(s32[1,256]{1,0:T(1,128)} %get-tuple-element.28.facing_ref) | copy-start | bytes 3076
  40.3 2.3 %collective-permute-start.5 = (bf16[288,128]{1,0:T(8,128)(2,1)S(1)}, bf16[288,128]{1,0:T(8,128)(2,1)S(1)}, u32[]{:S(2)}, u32[]{:S(2)}) collective-permute-start(bf16[288,128]{1,0:T(8,128)(2,1)S(1)} %get-tuple-element.30), channel_id=1, source_target_pairs={{0,1},{1,0},{2,3},{3,2},{4,5},{5,4},{6,7},{7,6},{8,9},{9,8},{10,11... | collective-permute-start | bytes 221192 | tf_op jit(solution)/shard_map/ppermute | solution.py:336
  40.4 5.1 %collective-permute-start.6 = (bf16[288,128]{1,0:T(8,128)(2,1)S(1)}, bf16[288,128]{1,0:T(8,128)(2,1)S(1)}, u32[]{:S(2)}, u32[]{:S(2)}) collective-permute-start(bf16[288,128]{1,0:T(8,128)(2,1)S(1)} %get-tuple-element.31), channel_id=1, source_target_pairs={{0,2},{1,3},{2,0},{3,1},{4,6},{5,7},{6,4},{7,5},{8,10},{9,11},{10,... | collective-permute-start | bytes 221192 | tf_op jit(solution)/shard_map/ppermute | solution.py:336
  40.4 5.7 %collective-permute-start.7 = (bf16[288,128]{1,0:T(8,128)(2,1)S(1)}, bf16[288,128]{1,0:T(8,128)(2,1)S(1)}, u32[]{:S(2)}, u32[]{:S(2)}) collective-permute-start(bf16[288,128]{1,0:T(8,128)(2,1)S(1)} %get-tuple-element.32), channel_id=1, source_target_pairs={{0,3},{1,2},{2,1},{3,0},{4,7},{5,6},{6,5},{7,4},{8,11},{9,10},{10,... | collective-permute-start | bytes 221192 | tf_op jit(solution)/shard_map/ppermute | solution.py:336

commit v2 on v1

--- a/solution.py
+++ b/solution.py
@@ -69,7 +69,8 @@
 
 
 def silu(half):
-    return (half + half * jnp.tanh(half)).astype(BF16)
+    half = half.astype(BF16)
+    return half + half * jnp.tanh(half)
 
 
 def pack_kernel(dev_ref, state_ref, sten_ref, owner_ref, pay_ref):
@@ -173,12 +174,12 @@
     for t in range(3):
         w1s_ref[128 * t : 128 * t + taps, :] = w1_ref[taps * t : taps * (t + 1), :] * BF16(0.5)
     for i in range(wi_ref.shape[0]):
-        g = [wi_ref[i, ch * t : ch * (t + 1), :].astype(F32) for t in range(3)]
-        sides, middle = 0.25 * (g[0] + g[2]), 0.25 * g[1]
-        w_ref[4 * i] = (0.5 * g[0]).astype(BF16)
-        w_ref[4 * i + 1] = (sides + middle).astype(BF16)
-        w_ref[4 * i + 2] = (sides - middle).astype(BF16)
-        w_ref[4 * i + 3] = (0.5 * g[2]).astype(BF16)
+        g = [wi_ref[i, ch * t : ch * (t + 1), :] for t in range(3)]
+        sides, middle = (g[0] + g[2]) * BF16(0.25), g[1] * BF16(0.25)
+        w_ref[4 * i] = g[0] * BF16(0.5)
+        w_ref[4 * i + 1] = sides + middle
+        w_ref[4 * i + 2] = sides - middle
+        w_ref[4 * i + 3] = g[2] * BF16(0.5)
     w24 = jnp.concatenate([wl_ref[:, ch * t : ch * (t + 1)].astype(F32) for t in range(3)], axis=0).astype(BF16)
 
     me = lax.rem(dev_ref[0], GROUP)

time: 47.7 us -> 42.1 us (0.88); the launches traced: 47.6 us -> 41.5 us
  Pallas kernels: 30.5 us -> 24.5 us
    pallas_call x1, Pallas kernels: 22 us -> 15.9 us  [per_device(): pl.pallas_call(functools.partial(net_kernel, levels, fields), out_shape=[...]
  transfers between devices with their start and end apart: 8 -> 8, of which waited for: 3 -> 3; matrix products, arithmetic and copies ran while one was open for 0% -> 0% of each run, Pallas kernels for 57% -> 51%
where the time goes in v2:
time: 42.1 us; the launch traced here: 41.5 us
  Pallas kernels  24.5 us (58%)
  starting transfers between devices  10.7 us (25%)
  waiting for transfers between devices  6.17 us (15%)
    pallas_call x1, Pallas kernels, per_device(): pl.pallas_call(functools.partial(net_kernel, levels, fields), out_shape=[...  15.9 us
    ppermute x6, waiting for transfers between devices, trade(): return lax.ppermute(x, AXES, [(i, i ^ d) for i in range(devices)])  6.17 us
    ppermute x1, starting transfers between devices, per_device(): lax.ppermute(edges, AXES, [(i, (i - 1) % devices) for i in range(devices)])  5.34 us
    ppermute x6, starting transfers between devices, trade(): return lax.ppermute(x, AXES, [(i, i ^ d) for i in range(devices)])  4.87 us
    pallas_call x1, Pallas kernels, per_device(): pl.pallas_call(functools.partial(edges_kernel, total), out_shape=(f32((ro...  4.83 us
    pallas_call x1, Pallas kernels, per_device(): pl.pallas_call(pack_kernel, out_shape=bf16((rows + 16, columns)), in_spec...  1.98 us
    pallas_call x1, Pallas kernels, per_device(): pl.pallas_call(final_kernel, out_shape=f32((fields, levels, columns)), in...  1.43 us
  transfers between devices with their start and end apart: 8, of which 3 were waited for; matrix products, arithmetic and copies ran while one was open for 0% of the time, Pallas kernels for 51%

profile of v2, /device:TPU:0, one launch (start us, length us, event | category | flops | bytes accessed | tf_op | source)
XLA Modules:
  0.0 41.5 jit_solution(4172540199884501464)
XLA Ops:
  0.0 2.0 %pack.1.m0_ref = bf16[592,256]{1,0:T(8,128)(2,1)} custom-call(s32[1]{0:T(128)} %bitcast.dev_ref, f32[8,72,256]{2,1,0:T(8,128)} %state_ref.3, s32[9,256]{1,0:T(8,128)} %bitcast.9, s32[1,256]{1,0:T(1,128)} %bitcast.10), custom_call_target="tpu_custom_call" | custom-call | tf_op jit(solution)/shard_map/pack/pallas_call | solution.py:329
  2.0 2.9 %collective-permute-start = (bf16[592,256]{1,0:T(8,128)(2,1)}, bf16[592,256]{1,0:T(8,128)(2,1)S(1)}, u32[]{:S(2)}, u32[]{:S(2)}) collective-permute-start(bf16[592,256]{1,0:T(8,128)(2,1)} %pack.1.m0_ref), channel_id=1, source_target_pairs={{0,2},{1,3},{2,0},{3,1},{4,6},{5,7},{6,4},{7,5},{8,10},{9,11},{10,... | collective-permute-start | bytes 909320 | tf_op jit(solution)/shard_map/ppermute | solution.py:337
  4.9 0.0 collective-permute-start.3
  4.9 0.0 copy-start
  4.9 0.0 copy-start.1
  4.9 0.0 copy-start.2
  4.9 0.0 copy-start.3
  4.9 4.8 %edges.1 = (f32[576,256]{1,0:T(8,128)}, bf16[576,128]{1,0:T(8,128)(2,1)}, s32[1,256]{1,0:T(1,128)}) custom-call(s32[1]{0:T(128)} %bitcast.dev_ref, f32[8,72,256]{2,1,0:T(8,128)} %state_ref.3, f32[1,256]{1,0:T(1,128)} %bitcast.12, f32[256,256]{1,0:T(8,128)} %constant.18.clone.op_ref, f32[256,128]{1,0:T(8,128)} %constant.19.clone.sel_ref, s32[4,16]{1,0:T(4,128)} %bitcast.11, ...), custom_call_target="tpu_custom_call" | custom-call | flops 3000000000 | bytes 2097152 | tf_op jit(solution)/shard_map/edges/pallas_call | solution.py:342
  9.8 2.5 %collective-permute-done.m2_ref = bf16[592,256]{1,0:T(8,128)(2,1)S(1)} collective-permute-done((bf16[592,256]{1,0:T(8,128)(2,1)}, bf16[592,256]{1,0:T(8,128)(2,1)S(1)}, u32[]{:S(2)}, u32[]{:S(2)}) %collective-permute-start) | collective-permute-done | bytes 303136 | tf_op jit(solution)/shard_map/ppermute | solution.py:337
  12.3 0.0 collective-permute-start.4
  12.3 0.5 %collective-permute-start.1 = (bf16[576,128]{1,0:T(8,128)(2,1)}, bf16[576,128]{1,0:T(8,128)(2,1)S(1)}, u32[]{:S(2)}, u32[]{:S(2)}) collective-permute-start(bf16[576,128]{1,0:T(8,128)(2,1)} %get-tuple-element.21), channel_id=1, source_target_pairs={{0,1},{1,2},{2,3},{3,4},{4,5},{5,6},{6,7},{7,8},{8,9},{9,10},{10,1... | collective-permute-start | bytes 442376 | tf_op jit(solution)/shard_map/ppermute | solution.py:354
  12.8 5.3 %collective-permute-start.2 = (bf16[576,128]{1,0:T(8,128)(2,1)}, bf16[576,128]{1,0:T(8,128)(2,1)S(1)}, u32[]{:S(2)}, u32[]{:S(2)}) collective-permute-start(bf16[576,128]{1,0:T(8,128)(2,1)} %get-tuple-element.21), channel_id=1, source_target_pairs={{0,31},{1,0},{2,1},{3,2},{4,3},{5,4},{6,5},{7,6},{8,7},{9,8},{10,9... | collective-permute-start | bytes 442376 | tf_op jit(solution)/shard_map/ppermute | solution.py:355
  18.2 0.0 collective-permute-done.3.m1_ref
  18.2 0.0 collective-permute-done.4.m3_ref
  18.2 0.0 copy-done
  18.2 0.0 copy-done.1
  18.2 0.0 copy-done.2
  18.2 0.0 copy-done.3
  18.2 0.0 copy-start.4
  18.2 0.0 copy-start.5
  18.2 15.9 %network.1 = (bf16[288,128]{1,0:T(8,128)(2,1)S(1)}, bf16[288,128]{1,0:T(8,128)(2,1)S(1)}, bf16[288,128]{1,0:T(8,128)(2,1)S(1)}, bf16[288,128]{1,0:T(8,128)(2,1)S(1)}, s32[1,256]{1,0:T(1,128)S(1)}) custom-call(s32[1]{0:T(128)} %bitcast.dev_ref, bf16[592,256]{1,0:T(8,128)(2,1)S(1)} %copy-done, bf16[592,256]{1,0:T(8,128)(2,1)S(1)} %collective-permute-done.3.m1_ref, ...), custom_call_target="tpu_custom_call" | custom-call | flops 10000000000 | bytes 4194304 | tf_op jit(solution)/shard_map/network/pallas_call | solution.py:359
  34.2 0.0 collective-permute-done.1.low_ref
  34.2 0.0 collective-permute-done.2.high_ref
  34.2 0.1 collective-permute-start.5
  34.3 0.1 collective-permute-start.6
  34.4 1.8 %collective-permute-start.7 = (bf16[288,128]{1,0:T(8,128)(2,1)S(1)}, bf16[288,128]{1,0:T(8,128)(2,1)S(1)}, u32[]{:S(2)}, u32[]{:S(2)}) collective-permute-start(bf16[288,128]{1,0:T(8,128)(2,1)S(1)} %get-tuple-element.32), channel_id=1, source_target_pairs={{0,3},{1,2},{2,1},{3,0},{4,7},{5,6},{6,5},{7,4},{8,11},{9,10},{10,... | collective-permute-start | bytes 221192 | tf_op jit(solution)/shard_map/ppermute | solution.py:337
  36.1 0.0 copy-done.4
  36.1 0.0 copy-done.5
  36.1 0.3 middle.1
  36.4 0.0 collective-permute-done.5.r1_ref
  36.5 2.9 %collective-permute-done.6.r2_ref = bf16[288,128]{1,0:T(8,128)(2,1)S(1)} collective-permute-done((bf16[288,128]{1,0:T(8,128)(2,1)S(1)}, bf16[288,128]{1,0:T(8,128)(2,1)S(1)}, u32[]{:S(2)}, u32[]{:S(2)}) %collective-permute-start.6) | collective-permute-done | bytes 73760 | tf_op jit(solution)/shard_map/ppermute | solution.py:337
  39.4 0.7 %collective-permute-done.7.r3_ref = bf16[288,128]{1,0:T(8,128)(2,1)S(1)} collective-permute-done((bf16[288,128]{1,0:T(8,128)(2,1)S(1)}, bf16[288,128]{1,0:T(8,128)(2,1)S(1)}, u32[]{:S(2)}, u32[]{:S(2)}) %collective-permute-start.7) | collective-permute-done | bytes 73760 | tf_op jit(solution)/shard_map/ppermute | solution.py:337
  40.1 1.4 %combine.1 = f32[8,72,256]{2,1,0:T(8,128)} custom-call(f32[8,72,256]{2,1,0:T(8,128)S(1)} %bitcast.7, s32[1,256]{1,0:T(1,128)S(1)} %get-tuple-element.29.code_ref, bf16[288,128]{1,0:T(8,128)(2,1)S(1)} %get-tuple-element.24.r0_ref, bf16[288,128]{1,0:T(8,128)(2,1)S(1)} %collective-permute-done.5.r1_ref, bf16[288,128]{1,0:T(8,128)(2,1)S(1)} %collective-permute-done.6.r2_ref, ...), custom_call_target="tpu_custom_call" | custom-call | tf_op jit(solution)/shard_map/combine/pallas_call | solution.py:398
Async XLA Ops:
  2.0 10.3 %collective-permute-start = (bf16[592,256]{1,0:T(8,128)(2,1)}, bf16[592,256]{1,0:T(8,128)(2,1)S(1)}, u32[]{:S(2)}, u32[]{:S(2)}) collective-permute-start(bf16[592,256]{1,0:T(8,128)(2,1)} %pack.1.m0_ref), channel_id=1, source_target_pairs={{0,2},{1,3},{2,0},{3,1},{4,6},{5,7},{6,4},{7,5},{8,10},{9,11},{10,... | collective-permute-start | bytes 909320 | tf_op jit(solution)/shard_map/ppermute | solution.py:337
  4.9 13.2 %collective-permute-start.3 = (bf16[592,256]{1,0:T(8,128)(2,1)}, bf16[592,256]{1,0:T(8,128)(2,1)S(1)}, u32[]{:S(2)}, u32[]{:S(2)}) collective-permute-start(bf16[592,256]{1,0:T(8,128)(2,1)} %pack.1.m0_ref), channel_id=1, source_target_pairs={{0,1},{1,0},{2,3},{3,2},{4,5},{5,4},{6,7},{7,6},{8,9},{9,8},{10,11... | collective-permute-start | bytes 909320 | tf_op jit(solution)/shard_map/ppermute | solution.py:337
  4.9 13.3 %copy-start = (bf16[592,256]{1,0:T(8,128)(2,1)S(1)}, bf16[592,256]{1,0:T(8,128)(2,1)}, u32[]{:S(2)}) copy-start(bf16[592,256]{1,0:T(8,128)(2,1)} %pack.1.m0_ref) | copy-start | bytes 909316
  4.9 13.3 %copy-start.1 = (bf16[5,768,256]{2,1,0:T(8,128)(2,1)S(1)}, bf16[5,768,256]{2,1,0:T(8,128)(2,1)}, u32[]{:S(2)}) copy-start(bf16[5,768,256]{2,1,0:T(8,128)(2,1)} %wi_ref.1) | copy-start | bytes 5898244
  4.9 13.3 %copy-start.2 = (bf16[216,256]{1,0:T(8,128)(2,1)S(1)}, bf16[216,256]{1,0:T(8,128)(2,1)}, u32[]{:S(2)}) copy-start(bf16[216,256]{1,0:T(8,128)(2,1)} %w1_ref.1) | copy-start | bytes 331780
  4.9 13.3 %copy-start.3 = (bf16[768,8]{0,1:T(8,128)(2,1)S(1)}, bf16[768,8]{0,1:T(8,128)(2,1)}, u32[]{:S(2)}) copy-start(bf16[768,8]{0,1:T(8,128)(2,1)} %param.19) | copy-start | bytes 36868
  12.3 5.9 %collective-permute-start.4 = (bf16[592,256]{1,0:T(8,128)(2,1)S(1)}, bf16[592,256]{1,0:T(8,128)(2,1)S(1)}, u32[]{:S(2)}, u32[]{:S(2)}) collective-permute-start(bf16[592,256]{1,0:T(8,128)(2,1)S(1)} %collective-permute-done.m2_ref), channel_id=1, source_target_pairs={{0,1},{1,0},{2,3},{3,2},{4,5},{5,4},{6,7},{7,6},{8,9},{9,8},{10,11... | collective-permute-start | bytes 909320 | tf_op jit(solution)/shard_map/ppermute | solution.py:337
  12.3 21.9 %collective-permute-start.1 = (bf16[576,128]{1,0:T(8,128)(2,1)}, bf16[576,128]{1,0:T(8,128)(2,1)S(1)}, u32[]{:S(2)}, u32[]{:S(2)}) collective-permute-start(bf16[576,128]{1,0:T(8,128)(2,1)} %get-tuple-element.21), channel_id=1, source_target_pairs={{0,1},{1,2},{2,3},{3,4},{4,5},{5,6},{6,7},{7,8},{8,9},{9,10},{10,1... | collective-permute-start | bytes 442376 | tf_op jit(solution)/shard_map/ppermute | solution.py:354
  12.8 21.4 %collective-permute-start.2 = (bf16[576,128]{1,0:T(8,128)(2,1)}, bf16[576,128]{1,0:T(8,128)(2,1)S(1)}, u32[]{:S(2)}, u32[]{:S(2)}) collective-permute-start(bf16[576,128]{1,0:T(8,128)(2,1)} %get-tuple-element.21), channel_id=1, source_target_pairs={{0,31},{1,0},{2,1},{3,2},{4,3},{5,4},{6,5},{7,6},{8,7},{9,8},{10,9... | collective-permute-start | bytes 442376 | tf_op jit(solution)/shard_map/ppermute | solution.py:355
  18.2 17.9 %copy-start.4 = (f32[576,256]{1,0:T(8,128)S(1)}, f32[576,256]{1,0:T(8,128)}, u32[]{:S(2)}) copy-start(f32[576,256]{1,0:T(8,128)} %get-tuple-element.25.base_ref) | copy-start | bytes 1769476
  18.2 17.9 %copy-start.5 = (s32[1,256]{1,0:T(1,128)S(1)}, s32[1,256]{1,0:T(1,128)}, u32[]{:S(2)}) copy-start(s32[1,256]{1,0:T(1,128)} %get-tuple-element.28.facing_ref) | copy-start | bytes 3076
  34.2 2.3 %collective-permute-start.5 = (bf16[288,128]{1,0:T(8,128)(2,1)S(1)}, bf16[288,128]{1,0:T(8,128)(2,1)S(1)}, u32[]{:S(2)}, u32[]{:S(2)}) collective-permute-start(bf16[288,128]{1,0:T(8,128)(2,1)S(1)} %get-tuple-element.30), channel_id=1, source_target_pairs={{0,1},{1,0},{2,3},{3,2},{4,5},{5,4},{6,7},{7,6},{8,9},{9,8},{10,11... | collective-permute-start | bytes 221192 | tf_op jit(solution)/shard_map/ppermute | solution.py:337
  34.3 5.1 %collective-permute-start.6 = (bf16[288,128]{1,0:T(8,128)(2,1)S(1)}, bf16[288,128]{1,0:T(8,128)(2,1)S(1)}, u32[]{:S(2)}, u32[]{:S(2)}) collective-permute-start(bf16[288,128]{1,0:T(8,128)(2,1)S(1)} %get-tuple-element.31), channel_id=1, source_target_pairs={{0,2},{1,3},{2,0},{3,1},{4,6},{5,7},{6,4},{7,5},{8,10},{9,11},{10,... | collective-permute-start | bytes 221192 | tf_op jit(solution)/shard_map/ppermute | solution.py:337
  34.4 5.7 %collective-permute-start.7 = (bf16[288,128]{1,0:T(8,128)(2,1)S(1)}, bf16[288,128]{1,0:T(8,128)(2,1)S(1)}, u32[]{:S(2)}, u32[]{:S(2)}) collective-permute-start(bf16[288,128]{1,0:T(8,128)(2,1)S(1)} %get-tuple-element.32), channel_id=1, source_target_pairs={{0,3},{1,2},{2,1},{3,0},{4,7},{5,6},{6,5},{7,4},{8,11},{9,10},{10,... | collective-permute-start | bytes 221192 | tf_op jit(solution)/shard_map/ppermute | solution.py:337
